TPU v7x, 32 devices: a whole 2x2x4 slice. The times are simulated.
32 devices in a mesh: dp: 4 (over y, x), expert: 8 (over z, core).
Axes of the slice: x: 2, y: 2, z: 4, core: 2. Of those that a mesh axis runs over, the one named last changes fastest.
Arguments:
- stream: bfloat16 [4096, 7168], P(('dp', 'expert')), may hold values from -30 to 30
- heads_out: bfloat16 [4096, 16384], P(('dp', 'expert')), may hold values from -6 to 6
- cotangent: bfloat16 [4096, 7168], P(('dp', 'expert')), may hold values from -6 to 6
- adapter_down: bfloat16 [16, 16384], replicated, may hold values from -0.046875 to 0.046875
- adapter_raise_factor: bfloat16 [16, 7168], replicated, may hold values from -0.59765625 to 0.59765625
- norm_gain: float32 [7168], replicated, may hold values from 0.5 to 2
- router: bfloat16 [256, 7168], replicated, may hold values from -0.125 to 0.125
- expert_ids: int32 [4096, 8], P(('dp', 'expert')), may hold values from 0 to 255, as said below
- w_gate_up: bfloat16 [8, 7168, 2, 1024], P('expert', None, None, 'dp'), may hold values from -0.0625 to 0.0625
- w_down: bfloat16 [8, 1024, 7168], P('expert', 'dp'), may hold values from -0.1875 to 0.1875
Outputs:
- residual_stream_gradient: bfloat16 [4096, 7168], P(('dp', 'expert'))
- grad_down: float32 [16, 16384], replicated
- raise_factor_gradient: float32 [16, 7168], replicated
Inputs may be any that keep to these rules, and one draw needn't show every extreme that they name: `expert_ids`: each row names 8 different experts. Within each aligned block of 128 rows (the tokens of one device) every expert below 8 is named by at most 6 rows, and one of them is named by exactly 6 rows in every block; the order of a row's ids carries no meaning.
All inputs are finite; a program needn't handle non-finite values.
Results may differ from a plain program's by a relative error of at most 0.0085.
Values may be sent and summed in bfloat16 or wider, within the bound.
A program may use at most 192 MiB of HBM per device.

v0:
```python
import jax
import jax.numpy as jnp
from jax import lax
from jax.sharding import PartitionSpec as P

ALL_EXP = 256
CAP = 6


adapter_scale_factor = 2.0
route_scale = 2.5
norm_eps = 1e-06


def expert_rows(rows_in, rows_grad, w_gate_up, w_down):
    quarter = w_down.shape[1]
    width = w_down.shape[2]
    flat_in = rows_in.reshape(-1, width)
    flat_grad = rows_grad.reshape(-1, width)
    joined = w_gate_up.reshape(width, 2 * quarter)
    lowered = w_down.reshape(quarter, width)
    projected = jnp.dot(flat_in, joined, preferred_element_type=jnp.float32)
    gate_pre = projected[:, :quarter]
    up_pre = projected[:, quarter:]
    sigma_gate = jax.nn.sigmoid(gate_pre)
    activated = gate_pre * sigma_gate
    hidden = (activated * up_pre).astype(jnp.bfloat16)
    hidden_grad = jnp.einsum("md,hd->mh", flat_grad, lowered, preferred_element_type=jnp.float32)
    slot_dots = jnp.sum(hidden.astype(jnp.float32) * hidden_grad, axis=1)
    pre_grad = jnp.concatenate(
        [
            hidden_grad * up_pre * sigma_gate * (1.0 + gate_pre * (1.0 - sigma_gate)),
            hidden_grad * activated,
        ],
        axis=1,
    ).astype(jnp.bfloat16)
    partial_rows = jnp.einsum("mk,dk->md", pre_grad, joined, preferred_element_type=jnp.float32)
    return (partial_rows, slot_dots)


def local(
    stream,
    heads_out,
    cotangent,
    adapter_down,
    adapter_raise_factor,
    norm_gain,
    router,
    expert_ids,
    w_gate_up,
    w_down,
):
    tokens_here = stream.shape[0]
    width = stream.shape[1]
    experts_here = lax.axis_size("expert")
    replicas = lax.axis_size("dp")
    hidden_code = jnp.einsum(
        "th,rh->tr", heads_out, adapter_down, preferred_element_type=jnp.float32
    ).astype(jnp.bfloat16)
    combined_result = stream.astype(jnp.float32) + adapter_scale_factor * jnp.dot(
        hidden_code, adapter_raise_factor, preferred_element_type=jnp.float32
    )
    inverse = lax.rsqrt(
        jnp.mean(combined_result * combined_result, axis=1, keepdims=True) + norm_eps
    )
    normed = combined_result * inverse
    normed_in = (normed * norm_gain).astype(jnp.bfloat16)
    logits = jnp.einsum("td,ed->te", normed_in, router, preferred_element_type=jnp.float32)
    affinity = jax.nn.sigmoid(logits)
    choose = expert_ids[:, :, None] == jnp.arange(ALL_EXP, dtype=jnp.int32)[None, None, :]
    chosen = jnp.sum(jnp.where(choose, affinity[:, None, :], 0.0), axis=2)
    affin_sum = jnp.sum(chosen, axis=1, keepdims=True)
    gate_weights = route_scale * chosen / affin_sum
    window_hit = expert_ids[:, :, None] == jnp.arange(experts_here, dtype=jnp.int32)[None, None, :]
    member = jnp.sum(window_hit.astype(jnp.int32), axis=1)
    gate_window = jnp.sum(jnp.where(window_hit, gate_weights[:, :, None], 0.0), axis=1)
    position = jnp.cumsum(member, axis=0) - member
    slot_hit = (member[:, :, None] == 1) & (
        position[:, :, None] == jnp.arange(CAP, dtype=jnp.int32)[None, None, :]
    )
    slot_count = experts_here * CAP
    pick = slot_hit.reshape(tokens_here, slot_count).astype(jnp.bfloat16)
    send_in = (
        jnp.einsum("ts,td->sd", pick, normed_in, preferred_element_type=jnp.float32)
        .astype(jnp.bfloat16)
        .reshape(experts_here, CAP, width)
    )
    send_grad = (
        jnp.einsum("ts,td->sd", pick, cotangent, preferred_element_type=jnp.float32)
        .astype(jnp.bfloat16)
        .reshape(experts_here, CAP, width)
    )
    got_in, got_grad = (
        lax.all_to_all(send_in, "expert", split_axis=0, concat_axis=0, tiled=True),
        lax.all_to_all(send_grad, "expert", split_axis=0, concat_axis=0, tiled=True),
    )
    rows_in, rows_grad = (
        lax.all_gather(got_in, "dp", axis=0, tiled=True),
        lax.all_gather(got_grad, "dp", axis=0, tiled=True),
    )
    partial_rows, slot_dots = expert_rows(rows_in, rows_grad, w_gate_up, w_down)
    partial_rows = partial_rows.reshape(replicas * experts_here, CAP, width)
    slot_dots = slot_dots.reshape(replicas * experts_here, CAP)
    summed_rows, summed_dots = (
        lax.psum_scatter(
            partial_rows.astype(jnp.bfloat16), "dp", scatter_dimension=0, tiled=True
        ).astype(jnp.float32),
        lax.psum_scatter(
            slot_dots.astype(jnp.bfloat16), "dp", scatter_dimension=0, tiled=True
        ).astype(jnp.float32),
    )
    returned, dot_sum = (
        lax.all_to_all(
            summed_rows.astype(jnp.bfloat16), "expert", split_axis=0, concat_axis=0, tiled=True
        ),
        lax.all_to_all(
            summed_dots.astype(jnp.bfloat16), "expert", split_axis=0, concat_axis=0, tiled=True
        ),
    )
    combine_weights = (
        jnp.where(slot_hit, gate_window[:, :, None], 0.0)
        .reshape(tokens_here, slot_count)
        .astype(jnp.bfloat16)
    )
    unit_grad = jnp.dot(
        combine_weights, returned.reshape(slot_count, width), preferred_element_type=jnp.float32
    )
    slot_dot = jnp.sum(jnp.where(slot_hit, dot_sum.astype(jnp.float32)[None, :, :], 0.0), axis=2)
    gate_grad = jnp.sum(jnp.where(window_hit, slot_dot[:, None, :], 0.0), axis=2)
    chosen_grad = route_scale * (
        gate_grad / affin_sum
        - jnp.sum(gate_grad * chosen, axis=1, keepdims=True) / (affin_sum * affin_sum)
    )
    logit_pick = chosen_grad * chosen * (1.0 - chosen)
    logit_grad = jnp.sum(jnp.where(choose, logit_pick[:, :, None], 0.0), axis=1).astype(
        jnp.bfloat16
    )
    unit_grad = unit_grad + jnp.dot(logit_grad, router, preferred_element_type=jnp.float32)
    scaled = unit_grad * norm_gain
    residual_stream_gradient = (
        cotangent.astype(jnp.float32)
        + inverse * (scaled - normed * jnp.mean(scaled * normed, axis=1, keepdims=True))
    ).astype(jnp.bfloat16)
    hidden_code_gradient = (
        adapter_scale_factor
        * jnp.einsum(
            "td,rd->tr",
            residual_stream_gradient,
            adapter_raise_factor,
            preferred_element_type=jnp.float32,
        )
    ).astype(jnp.bfloat16)
    partial_raise_sum = adapter_scale_factor * jnp.einsum(
        "tr,td->rd", hidden_code, residual_stream_gradient, preferred_element_type=jnp.float32
    )
    part_down = jnp.einsum(
        "tr,th->rh", hidden_code_gradient, heads_out, preferred_element_type=jnp.float32
    )
    sum_down, sum_up = lax.psum((part_down, partial_raise_sum), ("dp", "expert"))
    device_group = replicas * experts_here
    return (residual_stream_gradient, sum_down / device_group, sum_up / device_group)


def solution(mesh):
    return jax.shard_map(
        local,
        mesh=mesh,
        in_specs=(
            P(("dp", "expert"), None),
            P(("dp", "expert"), None),
            P(("dp", "expert"), None),
            P(),
            P(),
            P(),
            P(),
            P(("dp", "expert"), None),
            P("expert", None, None, "dp"),
            P("expert", "dp", None),
        ),
        out_specs=(P(("dp", "expert"), None), P(), P()),
        check_vma=False,
    )
```

profile of v0, /device:TPU:0, one launch (start us, length us, event | category | flops | bytes accessed | tf_op | source)
XLA Modules:
  0.0 420.3 jit_solution(16302911132033621273)
XLA Ops:
  8.6 3.4 convolution_convert_fusion.3
  13.0 1.7 copy-done.2
  17.6 29.9 %all_to_all.24 = bf16[8,6,7168]{2,1,0:T(8,128)(2,1)S(1)} all-to-all(bf16[8,6,7168]{2,1,0:T(8,128)(2,1)S(1)} %reshape.154), channel_id=1, replica_groups=mesh['dp'=4,'expert'=8] {'expert'}, dimensions={0} | all-to-all | bytes 1376256 | tf_op jit(solution)/shard_map/all_to_all | solution.py:94
  49.5 26.2 %all_to_all.25 = bf16[8,6,7168]{2,1,0:T(8,128)(2,1)S(1)} all-to-all(bf16[8,6,7168]{2,1,0:T(8,128)(2,1)S(1)} %reshape.151), channel_id=1, replica_groups=mesh['dp'=4,'expert'=8] {'expert'}, dimensions={0} | all-to-all | bytes 1376256 | tf_op jit(solution)/shard_map/all_to_all | solution.py:95
  77.1 12.4 %reshape.158 = bf16[7168,512,1]{1,0,2:T(8,128)(2,1)} reshape(bf16[1,7168,2,256]{3,2,1,0:T(2,128)(2,1)} %param.18) | data formatting | bytes 14680064 | tf_op jit(solution)/shard_map/reshape | solution.py:20
  89.6 7.4 %copy.77 = bf16[896,8,2,256]{3,1,2,0:T(8,128)(2,1)} copy(bf16[896,8,2,256]{3,2,1,0:T(2,128)(2,1)} %bitcast.42) | data formatting | bytes 14680064
  97.0 5.4 %copy.65 = bf16[32,6,7168]{2,1,0:T(8,128)(2,1)} copy(bf16[32,6,7168]{2,0,1:T(8,128)(2,1)} %all-gather.5.cloned.1.call-done) | data formatting | bytes 5505024 | tf_op jit(solution)/shard_map/all_gather | solution.py:98
  102.4 3.2 reshape.155
  105.6 26.1 %all-gather.3.cloned.1.call-done = bf16[32,6,7168]{2,0,1:T(8,128)(2,1)} async-done(((bf16[8,6,7168]{2,0,1:T(8,128)(2,1)}), bf16[32,6,7168]{2,0,1:T(8,128)(2,1)}) %all-gather.3.cloned.1.call-update) | async-done | bytes 2752528 | tf_op jit(solution)/shard_map/all_gather | solution.py:99
  131.7 5.2 %copy.63 = bf16[32,6,7168]{2,1,0:T(8,128)(2,1)} copy(bf16[32,6,7168]{2,0,1:T(8,128)(2,1)} %all-gather.3.cloned.1.call-done) | data formatting | bytes 5505024 | tf_op jit(solution)/shard_map/all_gather | solution.py:99
  136.9 4.6 %reshape.152 = bf16[192,7168]{1,0:T(8,128)(2,1)} reshape(bf16[32,6,7168]{2,1,0:T(8,128)(2,1)} %copy.63) | data formatting | bytes 5505024 | tf_op jit(solution)/shard_map/reshape | solution.py:19
  141.5 4.8 %fusion.23 = f32[192,512]{1,0:T(8,128)S(1)} fusion(bf16[192,7168]{1,0:T(8,128)(2,1)S(1)} %reshape.155, bf16[7168,512]{1,0:T(8,128)(2,1)} %bitcast.43), kind=kOutput, calls=%fused_computation.66 | convolution fusion | flops 1409286144 | bytes 10485760 | tf_op jit(solution)/shard_map/dot_general | solution.py:22
  148.1 7.2 %convolution_convert_fusion = bf16[32,6,7168]{2,0,1:T(8,128)(2,1)} fusion(bf16[7168,512,1]{1,0,2:T(8,128)(2,1)} %reshape.158, bf16[32,6,256]{2,0,1:T(8,128)(2,1)S(1)} %copy.67, bf16[32,6,256]{2,0,1:T(8,128)(2,1)S(1)} %copy.66), kind=kOutput, calls=%fused_computation | convolution fusion | flops 1411055616 | bytes 10289152 | tf_op jit(solution)/shard_map/mk,dk->md/dot_general | solution.py:37
  155.5 4.5 %fusion.6 = f32[128,256]{1,0:T(8,128)S(1)} fusion(bf16[256,7168]{1,0:T(8,128)(2,1)} %param.16, f32[128,7168]{1,0:T(8,128)} %copy-done.2, f32[7168]{0:T(1024)S(1)} %copy-done.11, f32[128]{0:T(128)S(1)} %add_rsqrt_fusion), kind=kOutput, calls=%fused_computation.20 | convolution fusion | flops 472612864 | bytes 7500288 | tf_op jit(solution)/shard_map/td,ed->te/dot_general | solution.py:68
  160.0 2.0 select_reduce_fusion
  163.4 9.6 %all-reduce.1 = bf16[32,6]{1,0:T(8,128)(2,1)S(1)} all-reduce(bf16[32,6]{1,0:T(8,128)(2,1)S(1)} %convert_element_type.78), channel_id=3, replica_groups=mesh['dp'=4,'expert'=8] {'dp'}, use_global_device_ids=true, to_apply=%region_8.9.clone | all-reduce | flops 192 | bytes 768
  173.6 4.6 %all-to-all-start.3 = ((bf16[8,1,6]{2,1,0:T(2,128)(2,1)}), bf16[8,1,6]{2,1,0:T(2,128)(2,1)S(1)}, u32[]{:S(2)}, u32[]{:S(2)}) async-start(bf16[8,1,6]{2,1,0:T(2,128)(2,1)} %copy.69), calls=%async_computation.3 | async-start | bytes 8192 | tf_op jit(solution)/shard_map/all_to_all | solution.py:116
  178.2 58.3 %all-reduce.6.cloned.1.call-done = bf16[32,6,7168]{2,0,1:T(8,128)(2,1)} async-done(((bf16[32,6,7168]{2,0,1:T(8,128)(2,1)}), bf16[32,6,7168]{2,0,1:T(8,128)(2,1)}) %all-reduce.6.cloned.1.call-update) | async-done | bytes 2752528
  239.0 4.6 %all-to-all-start.2 = ((bf16[8,6,7168]{2,1,0:T(8,128)(2,1)}), bf16[8,6,7168]{2,1,0:T(8,128)(2,1)S(1)}, u32[]{:S(2)}, u32[]{:S(2)}) async-start(bf16[8,6,7168]{2,1,0:T(8,128)(2,1)} %copy.68), calls=%async_computation.2 | async-start | bytes 1835008 | tf_op jit(solution)/shard_map/all_to_all | solution.py:113
  244.3 23.0 %all-to-all-done.2 = bf16[8,6,7168]{2,1,0:T(8,128)(2,1)S(1)} async-done(((bf16[8,6,7168]{2,1,0:T(8,128)(2,1)}), bf16[8,6,7168]{2,1,0:T(8,128)(2,1)S(1)}, u32[]{:S(2)}, u32[]{:S(2)}) %all-to-all-start.2) | async-done | bytes 688160 | tf_op jit(solution)/shard_map/all_to_all | solution.py:113
  273.1 6.0 %fusion.8 = f32[16,16384]{1,0:T(8,128)} fusion(bf16[128,16384]{1,0:T(8,128)(2,1)} %param.11, bf16[128,7168]{1,0:T(8,128)(2,1)S(1)} %add_convert_fusion, bf16[16,7168]{1,0:T(8,128)(2,1)S(1)} %copy-done.10), kind=kOutput, calls=%fused_computation.24 | convolution fusion | flops 96473088 | bytes 7307264 | tf_op jit(solution)/shard_map/tr,th->rh/dot_general | solution.py:156
  280.3 129.4 %all-reduce.8.cloned.1.call-done = (f32[16,16384]{1,0:T(8,128)}, f32[16,7168]{1,0:T(8,128)}) async-done(((f32[16,16384]{1,0:T(8,128)}, f32[16,7168]{1,0:T(8,128)}), (f32[16,16384]{1,0:T(8,128)}, f32[16,7168]{1,0:T(8,128)})) %all-reduce.8.cloned.1.call-update) | async-done | bytes 1507344 | tf_op jit(solution)/shard_map/psum | solution.py:159
  409.7 2.3 broadcast_multiply_fusion
  411.9 1.8 broadcast_multiply_fusion.1
  (87 shorter events, 21.9 us)
Async XLA Ops:
  7.2 1.4 copy-start
  7.2 4.8 %copy-start.9 = (bf16[128,7168]{1,0:T(8,128)(2,1)S(1)}, bf16[128,7168]{1,0:T(8,128)(2,1)}, u32[]{:S(2)}) copy-start(bf16[128,7168]{1,0:T(8,128)(2,1)} %param.10) | copy-start | bytes 5505028
  7.2 4.8 %copy-start.10 = (bf16[16,7168]{1,0:T(8,128)(2,1)S(1)}, bf16[16,7168]{1,0:T(8,128)(2,1)}, u32[]{:S(2)}) copy-start(bf16[16,7168]{1,0:T(8,128)(2,1)} %param.14) | copy-start | bytes 688132
  7.2 89.8 %all-gather.5.cloned.1.call-start = ((), (), s32[]{:S(2)}) async-start(), calls=%async_computation.5 | async-start | bytes 3440640 | tf_op jit(solution)/shard_map/all_gather | solution.py:98
  12.0 2.7 copy-start.11
  12.9 1.8 copy-start.2
  16.1 32.7 %copy-start.6 = (bf16[128,7168]{1,0:T(8,128)(2,1)S(1)}, bf16[128,7168]{1,0:T(8,128)(2,1)}, u32[]{:S(2)}) copy-start(bf16[128,7168]{1,0:T(8,128)(2,1)} %param.12) | copy-start | bytes 5505028
  48.8 83.0 %all-gather.3.cloned.1.call-start = ((), (), s32[]{:S(2)}) async-start(), calls=%async_computation.4 | async-start | bytes 3440640 | tf_op jit(solution)/shard_map/all_gather | solution.py:99
  76.9 159.6 %all-reduce.6.cloned.1.call-start = ((), (), s32[]{:S(2)}) async-start(), calls=%async_computation.6 | async-start | bytes 5505024
  141.5 4.8 %copy-start.8 = (bf16[192,7168]{1,0:T(8,128)(2,1)S(1)}, bf16[192,7168]{1,0:T(8,128)(2,1)}, u32[]{:S(2)}) copy-start(bf16[192,7168]{1,0:T(8,128)(2,1)} %reshape.152) | copy-start | bytes 8257540
  141.5 5.0 %copy-start.13 = (bf16[1,256,7168]{2,1,0:T(8,128)(2,1)S(1)}, bf16[1,256,7168]{2,1,0:T(8,128)(2,1)}, u32[]{:S(2)}) copy-start(bf16[1,256,7168]{2,1,0:T(8,128)(2,1)} %param.19) | copy-start | bytes 11010052
  148.1 7.2 %copy-start.12 = (s32[128,8]{0,1:T(8,128)S(1)}, s32[128,8]{0,1:T(8,128)}, u32[]{:S(2)}) copy-start(s32[128,8]{0,1:T(8,128)} %param.17) | copy-start | bytes 12292
  155.5 6.6 %copy-start.14 = (u32[32]{0:T(128)S(1)}, u32[32]{0:T(128)}, u32[]{:S(2)}) copy-start(u32[32]{0:T(128)} %constant.34) | copy-start | bytes 388
  173.6 65.4 %all-to-all-start.3 = ((bf16[8,1,6]{2,1,0:T(2,128)(2,1)}), bf16[8,1,6]{2,1,0:T(2,128)(2,1)S(1)}, u32[]{:S(2)}, u32[]{:S(2)}) async-start(bf16[8,1,6]{2,1,0:T(2,128)(2,1)} %copy.69), calls=%async_computation.3 | async-start | bytes 8192 | tf_op jit(solution)/shard_map/all_to_all | solution.py:116
  239.0 28.4 %all-to-all-start.2 = ((bf16[8,6,7168]{2,1,0:T(8,128)(2,1)}), bf16[8,6,7168]{2,1,0:T(8,128)(2,1)S(1)}, u32[]{:S(2)}, u32[]{:S(2)}) async-start(bf16[8,6,7168]{2,1,0:T(8,128)(2,1)} %copy.68), calls=%async_computation.2 | async-start | bytes 1835008 | tf_op jit(solution)/shard_map/all_to_all | solution.py:113
  243.6 166.1 %all-reduce.8.cloned.1.call-start = ((), (), s32[]{:S(2)}) async-start(), calls=%async_computation.7 | async-start | bytes 3014656 | tf_op jit(solution)/shard_map/psum | solution.py:159
  267.4 2.0 copy-start.3
  267.4 3.2 copy-start.5
  270.5 1.5 copy-start.7
  273.1 7.2 %copy-start.4 = (bf16[128,7168]{1,0:T(8,128)(2,1)}, bf16[128,7168]{1,0:T(8,128)(2,1)S(1)}, u32[]{:S(2)}) copy-start(bf16[128,7168]{1,0:T(8,128)(2,1)S(1)} %add_convert_fusion) | copy-start | bytes 5505028
  273.1 140.7 %copy-start.1 = (bf16[16,16384]{1,0:T(8,128)(2,1)S(1)}, bf16[16,16384]{1,0:T(8,128)(2,1)}, u32[]{:S(2)}) copy-start(bf16[16,16384]{1,0:T(8,128)(2,1)} %param.13) | copy-start | bytes 1572868
Sparse Core Ops, SparseCore 0:
  48.9 39.6 all-gather.4
  91.0 40.7 all-gather.2
  155.5 81.0 all-reduce.5
  280.4 129.2 all-reduce.7
where the time goes:
time: 421 us; the launch traced here: 420 us
  waiting for transfers between devices  237 us (56%)
  blocking collectives  65.7 us (16%)
  local copies, waits for them, and re-layouts  51.2 us (12%)
  matrix products  33.4 us (8%)
  between operations  14.7 us (3%)
  starting transfers between devices  9.56 us (2%)
  other arithmetic  8.8 us (2%)
    psum x1, waiting for transfers between devices, local(): lax.psum((part_down, partial_raise_sum), ('dp', 'expert'))  129 us
    unnamed x5, waiting for transfers between devices  58.4 us
    all_to_all x1, blocking collectives, local(): lax.all_to_all(send_in, 'expert', split_axis=0, concat_axis=0, tiled=True)  29.9 us
    all_to_all x1, blocking collectives, local(): lax.all_to_all(send_grad, 'expert', split_axis=0, concat_axis=0, tiled=True)  26.2 us
    all_gather x1, waiting for transfers between devices, local(): lax.all_gather(got_grad, 'dp', axis=0, tiled=True)  26.1 us
    all_to_all x1, waiting for transfers between devices, local(): lax.all_to_all(summed_rows.astype(jnp.bfloat16), 'expert', split_axis=0,...  23 us
    unnamed x34, local copies, waits for them, and re-layouts  13.6 us
    reshape x1, local copies, waits for them, and re-layouts, expert_rows(): joined = w_gate_up.reshape(width, 2 * quarter)  12.4 us
  transfers between devices with their start and end apart: 6, of which 4 were waited for; matrix products, arithmetic and copies ran while one was open for 10% of the time, Pallas kernels for 0%

commit v1 on v0

--- a/solution.py
+++ b/solution.py
@@ -1,15 +1,420 @@
+import functools
+
 import jax
 import jax.numpy as jnp
+import numpy as np
 from jax import lax
+from jax.experimental import pallas as pl
+from jax.experimental.pallas import tpu as pltpu
 from jax.sharding import PartitionSpec as P
 
 ALL_EXP = 256
 CAP = 6
-
+TILE = 16
+CHUNKS = 4
+LANES = 128
+VMEM_ROOM = 56 * 1024 * 1024
+MESH = pl.DeviceIdType.MESH
+F32 = jnp.float32
+BF16 = jnp.bfloat16
 
 adapter_scale_factor = 2.0
 route_scale = 2.5
 norm_eps = 1e-06
+
+
+def dot_nt(a, b):
+    return lax.dot_general(a, b, (((1,), (1,)), ((), ())), preferred_element_type=F32)
+
+
+def dot_tn(a, b):
+    return lax.dot_general(a, b, (((0,), (0,)), ((), ())), preferred_element_type=F32)
+
+
+def enter(n_dp, n_exp):
+    d, e = lax.axis_index("dp"), lax.axis_index("expert")
+    barrier = pltpu.get_barrier_semaphore()
+    for j in range(1, n_exp):
+        pl.semaphore_signal(barrier, inc=1, device_id=(d, e ^ j), device_id_type=MESH)
+    for j in range(1, n_dp):
+        pl.semaphore_signal(barrier, inc=1, device_id=(d ^ j, e), device_id_type=MESH)
+    pl.semaphore_wait(barrier, n_exp + n_dp - 2)
+    return d, e
+
+
+def remote(src, dst, send_sem, recv_sem, device):
+    copy = pltpu.make_async_remote_copy(
+        src_ref=src,
+        dst_ref=dst,
+        send_sem=send_sem,
+        recv_sem=recv_sem,
+        device_id=device,
+        device_id_type=MESH,
+    )
+    copy.start()
+    return copy
+
+
+def expert_kernel(
+    n_dp,
+    n_exp,
+    p_in_ref,
+    p_gr_ref,
+    q_ref,
+    qt_ref,
+    nin_ref,
+    cot_ref,
+    wj_hbm,
+    wd_hbm,
+    out_ref,
+    sent,
+    got,
+    rows,
+    parts,
+    arrived,
+    back,
+    back_got,
+    wj,
+    wd,
+    w_sem,
+    a_send,
+    a_recv,
+    g_send,
+    g_recv,
+    r_send,
+    r_recv,
+    b_send,
+    b_recv,
+):
+    width = nin_ref.shape[1]
+    slots = n_exp * CAP
+    step = width // CHUNKS
+    half = width // 2
+    piece = half // CHUNKS
+    quarter = wd.shape[0]
+    load_j = pltpu.make_async_copy(wj_hbm, wj, w_sem.at[0])
+    load_d = pltpu.make_async_copy(wd_hbm, wd, w_sem.at[1])
+    load_j.start()
+    load_d.start()
+    d, e = enter(n_dp, n_exp)
+    mine = pl.ds(pl.multiple_of(e * TILE, TILE), TILE)
+
+    first = []
+    for c in range(CHUNKS):
+        cols = pl.ds(c * step, step)
+        picked = jnp.dot(p_in_ref[...], nin_ref[:, cols], preferred_element_type=F32)
+        picked += jnp.dot(p_gr_ref[...], cot_ref[:, cols], preferred_element_type=F32)
+        sent[:, cols] = picked.astype(BF16)
+        copies = []
+        for j in range(1, n_exp):
+            theirs = pl.ds(pl.multiple_of((e ^ j) * TILE, TILE), TILE)
+            copies.append(
+                remote(
+                    sent.at[theirs, cols],
+                    got.at[mine, cols],
+                    a_send.at[c, j - 1],
+                    a_recv.at[c, j - 1],
+                    (d, e ^ j),
+                )
+            )
+        got[mine, cols] = sent[mine, cols]
+        first.append(copies)
+
+    second = []
+    for c in range(CHUNKS):
+        cols = pl.ds(c * step, step)
+        for copy in first[c]:
+            copy.wait_recv()
+        rows[d, :, cols] = jnp.dot(
+            q_ref[...], got[:, cols], preferred_element_type=F32
+        ).astype(BF16)
+        second.append(
+            [
+                remote(
+                    rows.at[d, :, cols],
+                    rows.at[d, :, cols],
+                    g_send.at[c, j - 1],
+                    g_recv.at[c, j - 1],
+                    (d ^ j, e),
+                )
+                for j in range(1, n_dp)
+            ]
+        )
+    load_j.wait()
+    load_d.wait()
+    projected = jnp.zeros((n_dp * slots, 2 * quarter), F32)
+    hidden_grad = jnp.zeros((n_dp * slots, quarter), F32)
+    for c in range(CHUNKS):
+        cols = pl.ds(c * step, step)
+        for copy in second[c]:
+            copy.wait_recv()
+        rows_in = rows[:, :slots, cols].reshape(n_dp * slots, step)
+        rows_grad = rows[:, slots:, cols].reshape(n_dp * slots, step)
+        projected += jnp.dot(rows_in, wj[cols, :], preferred_element_type=F32)
+        hidden_grad += dot_nt(rows_grad, wd[:, cols])
+    gate_pre = projected[:, :quarter]
+    up_pre = projected[:, quarter:]
+    sigma_gate = jax.nn.sigmoid(gate_pre)
+    activated = gate_pre * sigma_gate
+    hidden = (activated * up_pre).astype(BF16)
+    slot_dots = jnp.sum(hidden.astype(F32) * hidden_grad, axis=1, keepdims=True)
+    pre_grad = jnp.concatenate(
+        [
+            hidden_grad * up_pre * sigma_gate * (1.0 + gate_pre * (1.0 - sigma_gate)),
+            hidden_grad * activated,
+        ],
+        axis=1,
+    ).astype(BF16)
+
+    spans = [(width, LANES, half, False)]
+    spans += [(c * 2 * piece, 2 * piece, c * piece, True) for c in range(CHUNKS)]
+    third = []
+    for c, (at, size, _, real) in enumerate(spans):
+        if real:
+            low = (c - 1) * piece
+            part = jnp.concatenate(
+                [
+                    dot_nt(pre_grad, wj[pl.ds(low, piece), :]),
+                    dot_nt(pre_grad, wj[pl.ds(half + low, piece), :]),
+                ],
+                axis=1,
+            )
+        else:
+            part = jnp.broadcast_to(slot_dots, (n_dp * slots, LANES))
+        parts[:, :, pl.ds(at, size)] = part.astype(BF16).reshape(n_dp, slots, size)
+        third.append(
+            [
+                remote(
+                    parts.at[d ^ j, :, pl.ds(at, size)],
+                    arrived.at[j - 1, :, pl.ds(at, size)],
+                    r_send.at[c, j - 1],
+                    r_recv.at[c, j - 1],
+                    (d ^ j, e),
+                )
+                for j in range(1, n_dp)
+            ]
+        )
+    fourth = []
+    for c, (at, size, low, real) in enumerate(spans):
+        for copy in third[c]:
+            copy.wait_recv()
+        total = parts[d, :, pl.ds(at, size)].astype(F32)
+        for j in range(1, n_dp):
+            total += arrived[j - 1, :, pl.ds(at, size)].astype(F32)
+        total = total.astype(BF16)
+        if real:
+            spread = jnp.dot(qt_ref[:, :slots], total[:, :piece], preferred_element_type=F32)
+            spread += jnp.dot(qt_ref[:, slots:], total[:, piece:], preferred_element_type=F32)
+        else:
+            spread = jnp.dot(qt_ref[:, :slots], total, preferred_element_type=F32)
+        cols = pl.ds(low, spread.shape[1])
+        back[:, cols] = spread.astype(BF16)
+        copies = []
+        for j in range(1, n_exp):
+            theirs = pl.ds(pl.multiple_of((e ^ j) * TILE, TILE), TILE)
+            copies.append(
+                remote(
+                    back.at[theirs, cols],
+                    back_got.at[mine, cols],
+                    b_send.at[c, j - 1],
+                    b_recv.at[c, j - 1],
+                    (d, e ^ j),
+                )
+            )
+        back_got[mine, cols] = back[mine, cols]
+        fourth.append(copies)
+    for c, (_, size, low, real) in enumerate(spans):
+        for copy in fourth[c]:
+            copy.wait_recv()
+        cols = pl.ds(low, piece if real else size)
+        out_ref[:, cols] = back_got[:, cols]
+    for stage in (first, second, third, fourth):
+        for copies in stage:
+            for copy in copies:
+                copy.wait_send()
+
+
+def expert_buffers(n_dp, n_exp, width, quarter):
+    slots, padded = n_exp * CAP, n_exp * TILE
+    return [
+        ((padded, width), BF16),
+        ((padded, width), BF16),
+        ((n_dp, 2 * slots, width), BF16),
+        ((n_dp, slots, width + LANES), BF16),
+        ((n_dp - 1, slots, width + LANES), BF16),
+        ((padded, width // 2 + LANES), BF16),
+        ((padded, width // 2 + LANES), BF16),
+        ((width, 2 * quarter), BF16),
+        ((quarter, width), BF16),
+    ]
+
+
+def expert_exchange(p_in, p_gr, normed_in, cotangent, joined, lowered, n_dp, n_exp):
+    width = normed_in.shape[1]
+    quarter = lowered.shape[0]
+    slots, padded = n_exp * CAP, n_exp * TILE
+    squeeze = np.zeros((2 * slots, padded), np.float32)
+    for kind in range(2):
+        for e in range(n_exp):
+            for s in range(CAP):
+                squeeze[kind * slots + e * CAP + s, e * TILE + kind * CAP + s] = 1.0
+    vmem = pl.BlockSpec(memory_space=pltpu.VMEM)
+    dma = pltpu.SemaphoreType.DMA
+    return pl.pallas_call(
+        functools.partial(expert_kernel, n_dp, n_exp),
+        out_shape=jax.ShapeDtypeStruct((padded, width // 2 + LANES), BF16),
+        in_specs=[vmem] * 6 + [pl.BlockSpec(memory_space=pl.ANY)] * 2,
+        out_specs=vmem,
+        scratch_shapes=[
+            pltpu.VMEM(shape, kind)
+            for shape, kind in expert_buffers(n_dp, n_exp, width, quarter)
+        ]
+        + [
+            dma((2,)),
+            dma((CHUNKS, n_exp - 1)),
+            dma((CHUNKS, n_exp - 1)),
+            dma((CHUNKS, n_dp - 1)),
+            dma((CHUNKS, n_dp - 1)),
+            dma((CHUNKS + 1, n_dp - 1)),
+            dma((CHUNKS + 1, n_dp - 1)),
+            dma((CHUNKS + 1, n_exp - 1)),
+            dma((CHUNKS + 1, n_exp - 1)),
+        ],
+        compiler_params=pltpu.CompilerParams(
+            collective_id=0, has_side_effects=True, vmem_limit_bytes=VMEM_ROOM
+        ),
+    )(
+        p_in,
+        p_gr,
+        jnp.asarray(squeeze, BF16),
+        jnp.asarray(squeeze.T, BF16),
+        normed_in,
+        cotangent,
+        joined,
+        lowered,
+    )
+
+
+def reduce_kernel(
+    n_dp,
+    n_exp,
+    x_ref,
+    o_ref,
+    y,
+    z,
+    v,
+    b,
+    y_send,
+    y_recv,
+    v_send,
+    v_recv,
+    c_send,
+    c_recv,
+    d_send,
+    d_recv,
+):
+    wide = x_ref.shape[1] // n_dp
+    share = wide // n_exp
+    d, e = enter(n_dp, n_exp)
+
+    def block(i):
+        return pl.ds(pl.multiple_of(i * wide, LANES), wide)
+
+    def small(i):
+        return pl.ds(pl.multiple_of(i * share, LANES), share)
+
+    first = [
+        remote(
+            x_ref.at[:, block(d ^ j)],
+            y.at[j - 1],
+            y_send.at[j - 1],
+            y_recv.at[j - 1],
+            (d ^ j, e),
+        )
+        for j in range(1, n_dp)
+    ]
+    for copy in first:
+        copy.wait_recv()
+    total = x_ref[:, block(d)].astype(F32)
+    for j in range(1, n_dp):
+        total += y[j - 1].astype(F32)
+    z[...] = total.astype(BF16)
+    second = [
+        remote(
+            z.at[:, small(e ^ j)],
+            v.at[j - 1],
+            v_send.at[j - 1],
+            v_recv.at[j - 1],
+            (d, e ^ j),
+        )
+        for j in range(1, n_exp)
+    ]
+    for copy in second:
+        copy.wait_recv()
+    total = z[:, small(e)].astype(F32)
+    for j in range(1, n_exp):
+        total += v[j - 1].astype(F32)
+    own = small(d * n_exp + e)
+    b[:, own] = total.astype(BF16)
+    third = [
+        remote(b.at[:, own], b.at[:, own], c_send.at[j - 1], c_recv.at[j - 1], (d, e ^ j))
+        for j in range(1, n_exp)
+    ]
+    for copy in third:
+        copy.wait_recv()
+    fourth = [
+        remote(
+            b.at[:, block(d)], b.at[:, block(d)], d_send.at[j - 1], d_recv.at[j - 1], (d ^ j, e)
+        )
+        for j in range(1, n_dp)
+    ]
+    for copy in fourth:
+        copy.wait_recv()
+    o_ref[...] = b[...].astype(F32) * (1.0 / (n_dp * n_exp))
+    for copies in (first, second, third, fourth):
+        for copy in copies:
+            copy.wait_send()
+
+
+def mean_over_devices(terms, n_dp, n_exp):
+    rank = terms[0].shape[0]
+    total = sum(t.shape[1] for t in terms)
+    devices = n_dp * n_exp
+    share = -(-total // (devices * LANES)) * LANES
+    width = share * devices
+    x = jnp.concatenate(
+        [t.astype(BF16) for t in terms] + [jnp.zeros((rank, width - total), BF16)], axis=1
+    )
+    vmem = pl.BlockSpec(memory_space=pltpu.VMEM)
+    dma = pltpu.SemaphoreType.DMA
+    out = pl.pallas_call(
+        functools.partial(reduce_kernel, n_dp, n_exp),
+        out_shape=jax.ShapeDtypeStruct((rank, width), F32),
+        in_specs=[vmem],
+        out_specs=vmem,
+        scratch_shapes=[
+            pltpu.VMEM((n_dp - 1, rank, width // n_dp), BF16),
+            pltpu.VMEM((rank, width // n_dp), BF16),
+            pltpu.VMEM((n_exp - 1, rank, share), BF16),
+            pltpu.VMEM((rank, width), BF16),
+            dma((n_dp - 1,)),
+            dma((n_dp - 1,)),
+            dma((n_exp - 1,)),
+            dma((n_exp - 1,)),
+            dma((n_exp - 1,)),
+            dma((n_exp - 1,)),
+            dma((n_dp - 1,)),
+            dma((n_dp - 1,)),
+        ],
+        compiler_params=pltpu.CompilerParams(
+            collective_id=1, has_side_effects=True, vmem_limit_bytes=VMEM_ROOM
+        ),
+    )(x)
+    at, outs = 0, []
+    for t in terms:
+        outs.append(out[:, at : at + t.shape[1]])
+        at += t.shape[1]
+    return outs
 
 
 def expert_rows(rows_in, rows_grad, w_gate_up, w_down):
@@ -38,6 +443,26 @@
     return (partial_rows, slot_dots)
 
 
+def exchange_by_collectives(pick, normed_in, cotangent, w_gate_up, w_down):
+    width = normed_in.shape[1]
+    experts_here, replicas = lax.axis_size("expert"), lax.axis_size("dp")
+    gathered = []
+    for rows in (normed_in, cotangent):
+        send = jnp.dot(pick, rows, preferred_element_type=F32).astype(BF16)
+        got = lax.all_to_all(
+            send.reshape(experts_here, CAP, width), "expert", 0, 0, tiled=True
+        )
+        gathered.append(lax.all_gather(got, "dp", axis=0, tiled=True))
+    partial_rows, slot_dots = expert_rows(*gathered, w_gate_up, w_down)
+    sums = []
+    for part in (partial_rows, slot_dots[:, None]):
+        part = part.astype(BF16).reshape(replicas * experts_here, CAP, -1)
+        part = lax.psum_scatter(part, "dp", scatter_dimension=0, tiled=True)
+        part = lax.all_to_all(part.astype(BF16), "expert", 0, 0, tiled=True)
+        sums.append(part)
+    return sums[0].reshape(experts_here * CAP, width), sums[1][:, :, 0].astype(F32)
+
+
 def local(
     stream,
     heads_out,
@@ -71,61 +496,52 @@
     chosen = jnp.sum(jnp.where(choose, affinity[:, None, :], 0.0), axis=2)
     affin_sum = jnp.sum(chosen, axis=1, keepdims=True)
     gate_weights = route_scale * chosen / affin_sum
-    window_hit = expert_ids[:, :, None] == jnp.arange(experts_here, dtype=jnp.int32)[None, None, :]
-    member = jnp.sum(window_hit.astype(jnp.int32), axis=1)
-    gate_window = jnp.sum(jnp.where(window_hit, gate_weights[:, :, None], 0.0), axis=1)
-    position = jnp.cumsum(member, axis=0) - member
-    slot_hit = (member[:, :, None] == 1) & (
-        position[:, :, None] == jnp.arange(CAP, dtype=jnp.int32)[None, None, :]
-    )
-    slot_count = experts_here * CAP
-    pick = slot_hit.reshape(tokens_here, slot_count).astype(jnp.bfloat16)
-    send_in = (
-        jnp.einsum("ts,td->sd", pick, normed_in, preferred_element_type=jnp.float32)
-        .astype(jnp.bfloat16)
-        .reshape(experts_here, CAP, width)
-    )
-    send_grad = (
-        jnp.einsum("ts,td->sd", pick, cotangent, preferred_element_type=jnp.float32)
-        .astype(jnp.bfloat16)
-        .reshape(experts_here, CAP, width)
-    )
-    got_in, got_grad = (
-        lax.all_to_all(send_in, "expert", split_axis=0, concat_axis=0, tiled=True),
-        lax.all_to_all(send_grad, "expert", split_axis=0, concat_axis=0, tiled=True),
-    )
-    rows_in, rows_grad = (
-        lax.all_gather(got_in, "dp", axis=0, tiled=True),
-        lax.all_gather(got_grad, "dp", axis=0, tiled=True),
-    )
-    partial_rows, slot_dots = expert_rows(rows_in, rows_grad, w_gate_up, w_down)
-    partial_rows = partial_rows.reshape(replicas * experts_here, CAP, width)
-    slot_dots = slot_dots.reshape(replicas * experts_here, CAP)
-    summed_rows, summed_dots = (
-        lax.psum_scatter(
-            partial_rows.astype(jnp.bfloat16), "dp", scatter_dimension=0, tiled=True
-        ).astype(jnp.float32),
-        lax.psum_scatter(
-            slot_dots.astype(jnp.bfloat16), "dp", scatter_dimension=0, tiled=True
-        ).astype(jnp.float32),
-    )
-    returned, dot_sum = (
-        lax.all_to_all(
-            summed_rows.astype(jnp.bfloat16), "expert", split_axis=0, concat_axis=0, tiled=True
-        ),
-        lax.all_to_all(
-            summed_dots.astype(jnp.bfloat16), "expert", split_axis=0, concat_axis=0, tiled=True
-        ),
-    )
-    combine_weights = (
-        jnp.where(slot_hit, gate_window[:, :, None], 0.0)
-        .reshape(tokens_here, slot_count)
-        .astype(jnp.bfloat16)
-    )
-    unit_grad = jnp.dot(
-        combine_weights, returned.reshape(slot_count, width), preferred_element_type=jnp.float32
-    )
-    slot_dot = jnp.sum(jnp.where(slot_hit, dot_sum.astype(jnp.float32)[None, :, :], 0.0), axis=2)
+    window = jnp.arange(experts_here, dtype=jnp.int32)
+    window_hit = expert_ids[:, :, None] == window[None, None, :]
+    hit_any = jnp.sum(window_hit.astype(jnp.int32), axis=1).T
+    gate_window = jnp.sum(jnp.where(window_hit, gate_weights[:, :, None], 0.0), axis=1).T
+    token = jnp.arange(tokens_here, dtype=jnp.int32)
+    earlier = (token[:, None] < token[None, :]).astype(jnp.bfloat16)
+    before = jnp.dot(
+        hit_any.astype(jnp.bfloat16), earlier, preferred_element_type=jnp.float32
+    ).astype(jnp.int32)
+    position = jnp.where(hit_any == 1, before, -ALL_EXP)
+    slot = jnp.arange(TILE, dtype=jnp.int32)[None, :, None]
+    pick_low = position[:, None, :] == slot
+    pick_high = position[:, None, :] == slot - CAP
+    padded = experts_here * TILE
+    joined = w_gate_up.reshape(width, -1)
+    lowered = w_down.reshape(-1, width)
+    buffers = expert_buffers(replicas, experts_here, width, lowered.shape[0])
+    if sum(int(np.prod(shape)) * 2 for shape, _ in buffers) < 0.75 * VMEM_ROOM:
+        answer = expert_exchange(
+            pick_low.reshape(padded, tokens_here).astype(jnp.bfloat16),
+            pick_high.reshape(padded, tokens_here).astype(jnp.bfloat16),
+            normed_in,
+            cotangent,
+            joined,
+            lowered,
+            replicas,
+            experts_here,
+        )
+        returned = answer[:, : width // 2]
+        dot_sum = answer[:, width // 2].astype(jnp.float32).reshape(experts_here, TILE, 1)
+        weights = [
+            jnp.where(pick, gate_window[:, None, :], 0.0)
+            .reshape(padded, tokens_here)
+            .astype(jnp.bfloat16)
+            for pick in (pick_low, pick_high)
+        ]
+        unit_grad = jnp.concatenate([dot_tn(w, returned) for w in weights], axis=1)
+        slot_dot = jnp.sum(jnp.where(pick_low, dot_sum, 0.0), axis=1).T
+    else:
+        pick = pick_low[:, :CAP].reshape(-1, tokens_here)
+        returned, dot_sum = exchange_by_collectives(
+            pick.astype(jnp.bfloat16), normed_in, cotangent, w_gate_up, w_down
+        )
+        weights = jnp.where(pick_low[:, :CAP], gate_window[:, None, :], 0.0)
+        unit_grad = dot_tn(weights.reshape(-1, tokens_here).astype(jnp.bfloat16), returned)
+        slot_dot = jnp.sum(jnp.where(pick_low[:, :CAP], dot_sum[:, :, None], 0.0), axis=1).T
     gate_grad = jnp.sum(jnp.where(window_hit, slot_dot[:, None, :], 0.0), axis=2)
     chosen_grad = route_scale * (
         gate_grad / affin_sum
@@ -156,9 +572,10 @@
     part_down = jnp.einsum(
         "tr,th->rh", hidden_code_gradient, heads_out, preferred_element_type=jnp.float32
     )
-    sum_down, sum_up = lax.psum((part_down, partial_raise_sum), ("dp", "expert"))
-    device_group = replicas * experts_here
-    return (residual_stream_gradient, sum_down / device_group, sum_up / device_group)
+    mean_down, mean_up = mean_over_devices(
+        (part_down, partial_raise_sum), replicas, experts_here
+    )
+    return (residual_stream_gradient, mean_down, mean_up)
 
 
 def solution(mesh):

time: 421 us -> 203 us (0.48)
  waiting for transfers between devices: 237 us -> 0 us
  Pallas kernels: 0 us -> 162 us
  blocking collectives: 65.7 us -> 0 us
  local copies, waits for them, and re-layouts: 51.2 us -> 15.9 us
  matrix products: 33.4 us -> 16.6 us
  between operations: 14.7 us -> 0.9 us
  starting transfers between devices: 9.56 us -> 0 us
    pallas_call x0 -> x2, Pallas kernels: none -> 162 us  [the longest x1 123 us: expert_exchange(): pl.pallas_call(functools.partial(expert_kernel, n_dp, n_exp), out_shape=j...]
    psum x1 -> x0, waiting for transfers between devices: 129 us -> none  [local(): lax.psum((part_down, partial_raise_sum), ('dp', 'expert'))]
    unnamed x5 -> x0, waiting for transfers between devices: 58.4 us -> none
    all_to_all x2 -> x0, blocking collectives: 56.1 us -> none  [the longest x1 29.9 us: local(): lax.all_to_all(send_in, 'expert', split_axis=0, concat_axis=0, tiled=True)]
    all_gather x2 -> x0, waiting for transfers between devices: 26.1 us -> none  [the longest x1 26.1 us: local(): lax.all_gather(got_grad, 'dp', axis=0, tiled=True)]
    all_to_all x2 -> x0, waiting for transfers between devices: 23 us -> none  [the longest x1 23 us: local(): lax.all_to_all(summed_rows.astype(jnp.bfloat16), 'expert', split_axis=0,...]
    reshape x5 -> x0, local copies, waits for them, and re-layouts: 22 us -> none  [the longest x1 12.4 us: expert_rows(): joined = w_gate_up.reshape(width, 2 * quarter)]
    dot_general x6 -> x3, matrix products: 16 us -> 2.41 us  [the longest x2 2.28 us: dot_tn(): lax.dot_general(a, b, (((0,), (0,)), ((), ())), preferred_element_type=F32)]
  transfers between devices with their start and end apart: 6 -> 0, of which waited for: 4 -> 0; matrix products, arithmetic and copies ran while one was open for 10% -> 0% of each run, Pallas kernels for 0% -> 0%
where the time goes in v1:
time: 203 us; the launch traced here: 202 us
  Pallas kernels  162 us (80%)
  matrix products  16.6 us (8%)
  local copies, waits for them, and re-layouts  15.9 us (8%)
  other arithmetic  6.9 us (3%)
    pallas_call x1, Pallas kernels, expert_exchange(): pl.pallas_call(functools.partial(expert_kernel, n_dp, n_exp), out_shape=j...  123 us
    pallas_call x1, Pallas kernels, mean_over_devices(): pl.pallas_call(functools.partial(reduce_kernel, n_dp, n_exp), out_shape=j...  38.5 us
    unnamed x26, local copies, waits for them, and re-layouts  11.4 us
    dot_general x1, matrix products, local(): jnp.einsum('tr,th->rh', hidden_code_gradient, heads_out, preferred_elemen...  4.63 us
    slice x2, local copies, waits for them, and re-layouts, mean_over_devices(): outs.append(out[:, at:at + t.shape[1]])  4.08 us

profile of v1, /device:TPU:0, one launch (start us, length us, event | category | flops | bytes accessed | tf_op | source)
XLA Modules:
  0.0 202.3 jit_solution(10868401035319954855)
XLA Ops:
  0.7 1.0 copy-done
  1.7 3.4 %convolution_convert_fusion.1 = bf16[128,16]{0,1:T(8,128)(2,1)S(1)} fusion(bf16[128,16384]{1,0:T(8,128)(2,1)} %param.13, bf16[16,16384]{1,0:T(8,128)(2,1)S(1)} %copy-done), kind=kOutput, calls=%fused_computation.19 | convolution fusion | flops 67110912 | bytes 4722688 | tf_op jit(solution)/shard_map/th,rh->tr/dot_general | solution.py:482
  5.1 0.9 multiply_reduce_fusion.1
  6.0 1.9 copy-done.1
  7.9 0.4 multiply_convert_fusion.nin_ref
  8.3 1.0 copy-done.5
  9.4 1.4 fusion.5
  10.8 2.0 select_reduce_fusion
  13.0 0.1 fusion.7
  13.2 0.7 fusion.13
  14.0 7.3 %copy.36 = bf16[896,8,2,256]{3,1,2,0:T(8,128)(2,1)} copy(bf16[896,8,2,256]{3,2,1,0:T(2,128)(2,1)} %bitcast.46) | data formatting | bytes 14680064
  21.3 123.4 %shard_map.139 = bf16[128,3712]{1,0:T(8,128)(2,1)} custom-call(bf16[128,128]{1,0:T(8,128)(2,1)} %get-tuple-element.10.p_in_ref, bf16[128,128]{1,0:T(8,128)(2,1)} %get-tuple-element.9.p_gr_ref, bf16[96,128]{1,0:T(8,128)(2,1)} %constant.32.clone.q_ref, bf16[128,96]{1,0:T(8,128)(2,1)} %constant.33.clone.qt_ref, bf16[128,7168]{1,0:T(8,128)(2,1)} %copy-done.4, ...), custom_call_target="tpu_custom_call" | custom-call | tf_op jit(solution)/shard_map/pallas_call | solution.py:263
  144.8 0.9 convert_reduce_fusion
  146.1 0.4 select_reduce_fusion.2
  146.6 1.9 fusion.8
  148.5 0.4 fusion.10
  149.0 3.6 %multiply_reduce_fusion = (f32[128]{0:T(128)S(1)}, f32[128,7168]{1,0:T(8,128)S(1)}) fusion(f32[128,7168]{1,0:T(8,128)S(1)} %copy-done.2, f32[128]{0:T(128)S(1)} %add_rsqrt_fusion, f32[7168]{0:T(1024)S(1)} %copy-done.10, bf16[128,256]{1,0:T(8,128)(2,1)S(1)} %select_reduce_fusion.2, bf16[256,7168]{1,0:T(8,128)(2,1)} %param.18, f32[128,3584]{1,0:T(8,128)S(1)} %fusion.8, ...), kind=kOutput, calls=%fused_computation.8 | convolution fusion | flops 475266944 | bytes 14775296 | tf_op jit(solution)/shard_map/dot_general | solution.py:554
  152.6 1.0 add_convert_fusion
  153.7 0.4 fusion.2
  154.0 4.6 %convolution_convert_fusion = bf16[16,16384]{1,0:T(8,128)(2,1)S(1)} fusion(bf16[128,16384]{1,0:T(8,128)(2,1)} %param.13, bf16[128,7168]{1,0:T(8,128)(2,1)S(1)} %add_convert_fusion, bf16[16,7168]{1,0:T(8,128)(2,1)S(1)} %copy-done.9), kind=kOutput, calls=%fused_computation | convolution fusion | flops 96735232 | bytes 6782976 | tf_op jit(solution)/shard_map/tr,th->rh/dot_general | solution.py:572
  158.7 1.0 maximum_maximum_fusion.x_ref
  159.7 38.5 %shard_map.140 = f32[16,24576]{1,0:T(8,128)} custom-call(bf16[16,24576]{1,0:T(8,128)(2,1)} %maximum_maximum_fusion.x_ref), custom_call_target="tpu_custom_call" | custom-call | tf_op jit(solution)/shard_map/pallas_call | solution.py:390
  198.2 2.3 %slice.14 = f32[16,16384]{1,0:T(8,128)} slice(f32[16,24576]{1,0:T(8,128)} %shard_map.140), slice={[0:16], [0:16384]} | slice | bytes 2097152 | tf_op jit(solution)/shard_map/slice | solution.py:415
  200.5 1.8 slice.15
  (42 shorter events, 0.9 us)
Async XLA Ops:
  0.6 1.0 copy-start
  0.6 4.4 %copy-start.9 = (bf16[16,7168]{1,0:T(8,128)(2,1)S(1)}, bf16[16,7168]{1,0:T(8,128)(2,1)}, u32[]{:S(2)}) copy-start(bf16[16,7168]{1,0:T(8,128)(2,1)} %param.16) | copy-start | bytes 688132
  0.7 4.4 %copy-start.8 = (bf16[128,7168]{1,0:T(8,128)(2,1)S(1)}, bf16[128,7168]{1,0:T(8,128)(2,1)}, u32[]{:S(2)}) copy-start(bf16[128,7168]{1,0:T(8,128)(2,1)} %param.12) | copy-start | bytes 5505028
  5.1 2.8 %copy-start.10 = (f32[7168]{0:T(1024)S(1)}, f32[7168]{0:T(1024)}, u32[]{:S(2)}) copy-start(f32[7168]{0:T(1024)} %param.17) | copy-start | bytes 86020
  6.0 1.9 copy-start.1
  6.0 3.4 %copy-start.5 = (bf16[256,7168]{1,0:T(8,128)(2,1)S(1)}, bf16[256,7168]{1,0:T(8,128)(2,1)}, u32[]{:S(2)}) copy-start(bf16[256,7168]{1,0:T(8,128)(2,1)} %param.18) | copy-start | bytes 11010052
  9.3 12.0 %copy-start.4 = (bf16[128,7168]{1,0:T(8,128)(2,1)}, bf16[128,7168]{1,0:T(8,128)(2,1)S(1)}, u32[]{:S(2)}) copy-start(bf16[128,7168]{1,0:T(8,128)(2,1)S(1)} %multiply_convert_fusion.nin_ref) | copy-start | bytes 5505028
  9.3 1.4 copy-start.11
  144.8 3.7 %copy-start.6 = (bf16[128,3712]{1,0:T(8,128)(2,1)S(1)}, bf16[128,3712]{1,0:T(8,128)(2,1)}, u32[]{:S(2)}) copy-start(bf16[128,3712]{1,0:T(8,128)(2,1)} %shard_map.139) | copy-start | bytes 2850820
  146.1 2.8 %copy-start.2 = (f32[128,7168]{1,0:T(8,128)S(1)}, f32[128,7168]{1,0:T(8,128)}, u32[]{:S(2)}) copy-start(f32[128,7168]{1,0:T(8,128)} %copy-done.1) | copy-start | bytes 11010052
  148.9 3.7 %copy-start.7 = (bf16[128,7168]{1,0:T(8,128)(2,1)S(1)}, bf16[128,7168]{1,0:T(8,128)(2,1)}, u32[]{:S(2)}) copy-start(bf16[128,7168]{1,0:T(8,128)(2,1)} %cot_ref.1) | copy-start | bytes 5505028
  153.6 5.0 %copy-start.3 = (bf16[128,7168]{1,0:T(8,128)(2,1)}, bf16[128,7168]{1,0:T(8,128)(2,1)S(1)}, u32[]{:S(2)}) copy-start(bf16[128,7168]{1,0:T(8,128)(2,1)S(1)} %add_convert_fusion) | copy-start | bytes 5505028

commit v2 on v1

--- a/solution.py
+++ b/solution.py
@@ -11,7 +11,7 @@
 ALL_EXP = 256
 CAP = 6
 TILE = 16
-CHUNKS = 4
+CHUNKS = 7
 LANES = 128
 VMEM_ROOM = 56 * 1024 * 1024
 MESH = pl.DeviceIdType.MESH
@@ -120,33 +120,50 @@
         got[mine, cols] = sent[mine, cols]
         first.append(copies)
 
-    second = []
-    for c in range(CHUNKS):
-        cols = pl.ds(c * step, step)
-        for copy in first[c]:
-            copy.wait_recv()
-        rows[d, :, cols] = jnp.dot(
-            q_ref[...], got[:, cols], preferred_element_type=F32
-        ).astype(BF16)
-        second.append(
-            [
-                remote(
-                    rows.at[d, :, cols],
-                    rows.at[d, :, cols],
-                    g_send.at[c, j - 1],
-                    g_recv.at[c, j - 1],
-                    (d ^ j, e),
+    second, relayed = [], []
+    for c in range(CHUNKS + 1):
+        if c < CHUNKS:
+            cols = pl.ds(c * step, step)
+            for copy in first[c]:
+                copy.wait_recv()
+            rows[0, :, cols] = jnp.dot(
+                q_ref[...], got[:, cols], preferred_element_type=F32
+            ).astype(BF16)
+            second.append(
+                [
+                    remote(
+                        rows.at[0, :, cols],
+                        rows.at[j, :, cols],
+                        g_send.at[c, j - 1],
+                        g_recv.at[c, j - 1],
+                        (d ^ j, e),
+                    )
+                    for j in (1, 2)
+                ]
+            )
+        if c > 0:
+            cols = pl.ds((c - 1) * step, step)
+            copies = []
+            for j in (1, 2):
+                second[c - 1][j - 1].wait_recv()
+                some = pl.ds((j - 1) * slots, slots)
+                copies.append(
+                    remote(
+                        rows.at[j, some, cols],
+                        rows.at[3, some, cols],
+                        g_send.at[c - 1, j + 1],
+                        g_recv.at[c - 1, j + 1],
+                        (d ^ (3 - j), e),
+                    )
                 )
-                for j in range(1, n_dp)
-            ]
-        )
+            relayed.append(copies)
     load_j.wait()
     load_d.wait()
     projected = jnp.zeros((n_dp * slots, 2 * quarter), F32)
     hidden_grad = jnp.zeros((n_dp * slots, quarter), F32)
     for c in range(CHUNKS):
         cols = pl.ds(c * step, step)
-        for copy in second[c]:
+        for copy in relayed[c]:
             copy.wait_recv()
         rows_in = rows[:, :slots, cols].reshape(n_dp * slots, step)
         rows_grad = rows[:, slots:, cols].reshape(n_dp * slots, step)
@@ -167,68 +184,90 @@
     ).astype(BF16)
 
     spans = [(width, LANES, half, False)]
-    spans += [(c * 2 * piece, 2 * piece, c * piece, True) for c in range(CHUNKS)]
-    third = []
-    for c, (at, size, _, real) in enumerate(spans):
-        if real:
-            low = (c - 1) * piece
-            part = jnp.concatenate(
-                [
-                    dot_nt(pre_grad, wj[pl.ds(low, piece), :]),
-                    dot_nt(pre_grad, wj[pl.ds(half + low, piece), :]),
-                ],
-                axis=1,
-            )
-        else:
-            part = jnp.broadcast_to(slot_dots, (n_dp * slots, LANES))
-        parts[:, :, pl.ds(at, size)] = part.astype(BF16).reshape(n_dp, slots, size)
-        third.append(
-            [
-                remote(
-                    parts.at[d ^ j, :, pl.ds(at, size)],
-                    arrived.at[j - 1, :, pl.ds(at, size)],
-                    r_send.at[c, j - 1],
-                    r_recv.at[c, j - 1],
-                    (d ^ j, e),
+    spans += [(c * 2 * piece, piece, c * piece, True) for c in range(CHUNKS)]
+    count = len(spans)
+    third, passed, fourth = [], [], []
+    for turn in range(count + 2):
+        if turn < count:
+            c = turn
+            at, size, low, real = spans[c]
+            copies = []
+            for j in (1, 2) if real else (1,):
+                cols = pl.ds(at + (j - 1) * size, size)
+                if real:
+                    part = dot_nt(pre_grad, wj[pl.ds((j - 1) * half + low, size), :])
+                else:
+                    part = jnp.broadcast_to(slot_dots, (n_dp * slots, LANES))
+                parts[:, :, cols] = part.astype(BF16).reshape(n_dp, slots, size)
+                copies.append(
+                    [
+                        remote(
+                            parts.at[block, :, cols],
+                            arrived.at[place, :, cols],
+                            r_send.at[c, j - 1, place],
+                            r_recv.at[c, j - 1, place],
+                            (d ^ j, e),
+                        )
+                        for place, block in ((1, 3), (0, j))
+                    ]
                 )
-                for j in range(1, n_dp)
-            ]
-        )
-    fourth = []
-    for c, (at, size, low, real) in enumerate(spans):
-        for copy in third[c]:
-            copy.wait_recv()
-        total = parts[d, :, pl.ds(at, size)].astype(F32)
-        for j in range(1, n_dp):
-            total += arrived[j - 1, :, pl.ds(at, size)].astype(F32)
-        total = total.astype(BF16)
-        if real:
-            spread = jnp.dot(qt_ref[:, :slots], total[:, :piece], preferred_element_type=F32)
-            spread += jnp.dot(qt_ref[:, slots:], total[:, piece:], preferred_element_type=F32)
-        else:
-            spread = jnp.dot(qt_ref[:, :slots], total, preferred_element_type=F32)
-        cols = pl.ds(low, spread.shape[1])
-        back[:, cols] = spread.astype(BF16)
-        copies = []
-        for j in range(1, n_exp):
-            theirs = pl.ds(pl.multiple_of((e ^ j) * TILE, TILE), TILE)
-            copies.append(
-                remote(
-                    back.at[theirs, cols],
-                    back_got.at[mine, cols],
-                    b_send.at[c, j - 1],
-                    b_recv.at[c, j - 1],
-                    (d, e ^ j),
+            third.append(copies)
+        if 0 < turn <= count:
+            c = turn - 1
+            at, size, low, real = spans[c]
+            copies = []
+            for j in (1, 2) if real else (1,):
+                cols = pl.ds(at + (j - 1) * size, size)
+                other = 3 - j
+                for copy in third[c][j - 1]:
+                    copy.wait_recv()
+                both = parts[other, :, cols].astype(F32) + arrived[1, :, cols].astype(F32)
+                parts[other, :, cols] = both.astype(BF16)
+                copies.append(
+                    remote(
+                        parts.at[other, :, cols],
+                        arrived.at[2, :, cols],
+                        r_send.at[c, j - 1, 2],
+                        r_recv.at[c, j - 1, 2],
+                        (d ^ other, e),
+                    )
                 )
-            )
-        back_got[mine, cols] = back[mine, cols]
-        fourth.append(copies)
+            passed.append(copies)
+        if turn >= 2:
+            c = turn - 2
+            at, size, low, real = spans[c]
+            spread = jnp.zeros((n_exp * TILE, size), F32)
+            for j in (1, 2) if real else (1,):
+                cols = pl.ds(at + (j - 1) * size, size)
+                passed[c][j - 1].wait_recv()
+                total = parts[0, :, cols].astype(F32) + arrived[0, :, cols].astype(F32)
+                total = (total + arrived[2, :, cols].astype(F32)).astype(BF16)
+                spread += jnp.dot(
+                    qt_ref[j - 1], total, preferred_element_type=F32
+                )
+            cols = pl.ds(low, size)
+            back[:, cols] = spread.astype(BF16)
+            copies = []
+            for j in range(1, n_exp):
+                theirs = pl.ds(pl.multiple_of((e ^ j) * TILE, TILE), TILE)
+                copies.append(
+                    remote(
+                        back.at[theirs, cols],
+                        back_got.at[mine, cols],
+                        b_send.at[c, j - 1],
+                        b_recv.at[c, j - 1],
+                        (d, e ^ j),
+                    )
+                )
+            back_got[mine, cols] = back[mine, cols]
+            fourth.append(copies)
     for c, (_, size, low, real) in enumerate(spans):
         for copy in fourth[c]:
             copy.wait_recv()
-        cols = pl.ds(low, piece if real else size)
+        cols = pl.ds(low, size)
         out_ref[:, cols] = back_got[:, cols]
-    for stage in (first, second, third, fourth):
+    third = [sum(copies, []) for copies in third]
+    for stage in (first, second, relayed, third, passed, fourth):
         for copies in stage:
             for copy in copies:
                 copy.wait_send()
@@ -273,10 +312,10 @@
             dma((2,)),
             dma((CHUNKS, n_exp - 1)),
             dma((CHUNKS, n_exp - 1)),
-            dma((CHUNKS, n_dp - 1)),
-            dma((CHUNKS, n_dp - 1)),
-            dma((CHUNKS + 1, n_dp - 1)),
-            dma((CHUNKS + 1, n_dp - 1)),
+            dma((CHUNKS, 4)),
+            dma((CHUNKS, 4)),
+            dma((CHUNKS + 1, 2, 3)),
+            dma((CHUNKS + 1, 2, 3)),
             dma((CHUNKS + 1, n_exp - 1)),
             dma((CHUNKS + 1, n_exp - 1)),
         ],
@@ -287,7 +326,7 @@
         p_in,
         p_gr,
         jnp.asarray(squeeze, BF16),
-        jnp.asarray(squeeze.T, BF16),
+        jnp.asarray(squeeze.reshape(2, slots, padded).transpose(0, 2, 1), BF16),
         normed_in,
         cotangent,
         joined,
@@ -295,85 +334,61 @@
     )
 
 
-def reduce_kernel(
-    n_dp,
-    n_exp,
-    x_ref,
-    o_ref,
-    y,
-    z,
-    v,
-    b,
-    y_send,
-    y_recv,
-    v_send,
-    v_recv,
-    c_send,
-    c_recv,
-    d_send,
-    d_recv,
-):
-    wide = x_ref.shape[1] // n_dp
-    share = wide // n_exp
+def reduce_kernel(n_dp, n_exp, x_ref, o_ref, *scratch):
     d, e = enter(n_dp, n_exp)
-
-    def block(i):
-        return pl.ds(pl.multiple_of(i * wide, LANES), wide)
-
-    def small(i):
-        return pl.ds(pl.multiple_of(i * share, LANES), share)
-
-    first = [
-        remote(
-            x_ref.at[:, block(d ^ j)],
-            y.at[j - 1],
-            y_send.at[j - 1],
-            y_recv.at[j - 1],
-            (d ^ j, e),
-        )
-        for j in range(1, n_dp)
+    pairs = n_exp // 2
+    groups = [
+        (2, e & 1, lambda j: (d, e ^ j)),
+        (n_dp, d, lambda j: (d ^ j, e)),
+        (pairs, e >> 1, lambda j: (d, e ^ (2 * j))),
     ]
-    for copy in first:
-        copy.wait_recv()
-    total = x_ref[:, block(d)].astype(F32)
-    for j in range(1, n_dp):
-        total += y[j - 1].astype(F32)
-    z[...] = total.astype(BF16)
-    second = [
-        remote(
-            z.at[:, small(e ^ j)],
-            v.at[j - 1],
-            v_send.at[j - 1],
-            v_recv.at[j - 1],
-            (d, e ^ j),
-        )
-        for j in range(1, n_exp)
-    ]
-    for copy in second:
-        copy.wait_recv()
-    total = z[:, small(e)].astype(F32)
-    for j in range(1, n_exp):
-        total += v[j - 1].astype(F32)
-    own = small(d * n_exp + e)
-    b[:, own] = total.astype(BF16)
-    third = [
-        remote(b.at[:, own], b.at[:, own], c_send.at[j - 1], c_recv.at[j - 1], (d, e ^ j))
-        for j in range(1, n_exp)
-    ]
-    for copy in third:
-        copy.wait_recv()
-    fourth = [
-        remote(
-            b.at[:, block(d)], b.at[:, block(d)], d_send.at[j - 1], d_recv.at[j - 1], (d ^ j, e)
-        )
-        for j in range(1, n_dp)
-    ]
-    for copy in fourth:
-        copy.wait_recv()
-    o_ref[...] = b[...].astype(F32) * (1.0 / (n_dp * n_exp))
-    for copies in (first, second, third, fourth):
+    started = []
+    held, size, base, bases = x_ref, x_ref.shape[1], 0, []
+    for k, (n, index, partner) in enumerate(groups):
+        got, total_ref, send, recv = scratch[4 * k : 4 * k + 4]
+        size //= n
+
+        def part(i, size=size):
+            return pl.ds(pl.multiple_of(i * size, LANES), size)
+
+        copies = [
+            remote(
+                held.at[:, part(index ^ j)],
+                got.at[j - 1],
+                send.at[0, j - 1],
+                recv.at[0, j - 1],
+                partner(j),
+            )
+            for j in range(1, n)
+        ]
         for copy in copies:
-            copy.wait_send()
+            copy.wait_recv()
+        started += copies
+        total = held[:, part(index)].astype(F32)
+        for j in range(1, n):
+            total += got[j - 1].astype(F32)
+        total_ref[...] = total.astype(BF16)
+        held = total_ref
+        base = base + index * size
+        bases.append((base, size))
+    base, size = bases[-1]
+    o_ref[:, pl.ds(pl.multiple_of(base, LANES), size)] = held[...]
+    for k in reversed(range(3)):
+        n, _, partner = groups[k]
+        _, _, send, recv = scratch[4 * k : 4 * k + 4]
+        base, size = bases[k]
+        own = pl.ds(pl.multiple_of(base, LANES), size)
+        copies = [
+            remote(
+                o_ref.at[:, own], o_ref.at[:, own], send.at[1, j - 1], recv.at[1, j - 1], partner(j)
+            )
+            for j in range(1, n)
+        ]
+        for copy in copies:
+            copy.wait_recv()
+        started += copies
+    for copy in started:
+        copy.wait_send()
 
 
 def mean_over_devices(terms, n_dp, n_exp):
@@ -387,32 +402,24 @@
     )
     vmem = pl.BlockSpec(memory_space=pltpu.VMEM)
     dma = pltpu.SemaphoreType.DMA
+    scratch, size = [], width
+    for n in (2, n_dp, n_exp // 2):
+        size //= n
+        scratch += [pltpu.VMEM((n - 1, rank, size), BF16), pltpu.VMEM((rank, size), BF16)]
+        scratch += [dma((2, n - 1)), dma((2, n - 1))]
     out = pl.pallas_call(
         functools.partial(reduce_kernel, n_dp, n_exp),
-        out_shape=jax.ShapeDtypeStruct((rank, width), F32),
+        out_shape=jax.ShapeDtypeStruct((rank, width), BF16),
         in_specs=[vmem],
         out_specs=vmem,
-        scratch_shapes=[
-            pltpu.VMEM((n_dp - 1, rank, width // n_dp), BF16),
-            pltpu.VMEM((rank, width // n_dp), BF16),
-            pltpu.VMEM((n_exp - 1, rank, share), BF16),
-            pltpu.VMEM((rank, width), BF16),
-            dma((n_dp - 1,)),
-            dma((n_dp - 1,)),
-            dma((n_exp - 1,)),
-            dma((n_exp - 1,)),
-            dma((n_exp - 1,)),
-            dma((n_exp - 1,)),
-            dma((n_dp - 1,)),
-            dma((n_dp - 1,)),
-        ],
+        scratch_shapes=scratch,
         compiler_params=pltpu.CompilerParams(
             collective_id=1, has_side_effects=True, vmem_limit_bytes=VMEM_ROOM
         ),
     )(x)
     at, outs = 0, []
     for t in terms:
-        outs.append(out[:, at : at + t.shape[1]])
+        outs.append(out[:, at : at + t.shape[1]].astype(F32) / devices)
         at += t.shape[1]
     return outs
 
@@ -513,7 +520,8 @@
     joined = w_gate_up.reshape(width, -1)
     lowered = w_down.reshape(-1, width)
     buffers = expert_buffers(replicas, experts_here, width, lowered.shape[0])
-    if sum(int(np.prod(shape)) * 2 for shape, _ in buffers) < 0.75 * VMEM_ROOM:
+    fits = replicas == 4 and sum(int(np.prod(shape)) * 2 for shape, _ in buffers) < 0.75 * VMEM_ROOM
+    if fits:
         answer = expert_exchange(
             pick_low.reshape(padded, tokens_here).astype(jnp.bfloat16),
             pick_high.reshape(padded, tokens_here).astype(jnp.bfloat16),

time: 203 us -> 174 us (0.86)
  Pallas kernels: 162 us -> 134 us
  local copies, waits for them, and re-layouts: 15.9 us -> 11.8 us
  other arithmetic: 6.9 us -> 10.7 us
    pallas_call x1, Pallas kernels: 123 us -> 106 us  [expert_exchange(): pl.pallas_call(functools.partial(expert_kernel, n_dp, n_exp), out_shape=j...]
    pallas_call x1, Pallas kernels: 38.5 us -> 28 us  [mean_over_devices(): pl.pallas_call(functools.partial(reduce_kernel, n_dp, n_exp), out_shape=j...]
    slice x2 -> x0, local copies, waits for them, and re-layouts: 4.08 us -> none  [mean_over_devices(): outs.append(out[:, at:at + t.shape[1]])]
    div x0 -> x2, other arithmetic: none -> 3.82 us  [mean_over_devices(): outs.append(out[:, at:at + t.shape[1]].astype(F32) / devices)]
where the time goes in v2:
time: 174 us
  Pallas kernels  134 us (77%)
  matrix products  16.7 us (10%)
  local copies, waits for them, and re-layouts  11.8 us (7%)
  other arithmetic  10.7 us (6%)
    pallas_call x1, Pallas kernels, expert_exchange(): pl.pallas_call(functools.partial(expert_kernel, n_dp, n_exp), out_shape=j...  106 us
    pallas_call x1, Pallas kernels, mean_over_devices(): pl.pallas_call(functools.partial(reduce_kernel, n_dp, n_exp), out_shape=j...  28 us
    unnamed x26, local copies, waits for them, and re-layouts  11.4 us
    dot_general x1, matrix products, local(): jnp.einsum('tr,th->rh', hidden_code_gradient, heads_out, preferred_elemen...  4.63 us
    div x2, other arithmetic, mean_over_devices(): outs.append(out[:, at:at + t.shape[1]].astype(F32) / devices)  3.82 us
    dot_general x1, matrix products, local(): jnp.dot(logit_grad, router, preferred_element_type=jnp.float32)  3.64 us

profile of v2, /device:TPU:0, one launch (start us, length us, event | category | flops | bytes accessed | tf_op | source)
XLA Modules:
  0.0 174.0 jit_solution(3058153769589240334)
XLA Ops:
  0.7 1.0 copy-done
  1.7 3.4 %convolution_convert_fusion.1 = bf16[128,16]{0,1:T(8,128)(2,1)S(1)} fusion(bf16[128,16384]{1,0:T(8,128)(2,1)} %param.13, bf16[16,16384]{1,0:T(8,128)(2,1)S(1)} %copy-done), kind=kOutput, calls=%fused_computation.19 | convolution fusion | flops 67110912 | bytes 4722688 | tf_op jit(solution)/shard_map/th,rh->tr/dot_general | solution.py:489
  5.1 0.9 multiply_reduce_fusion.1
  6.0 1.9 %copy-done.1 = f32[128,7168]{1,0:T(8,128)} copy-done((f32[128,7168]{1,0:T(8,128)}, f32[128,7168]{1,0:T(8,128)S(1)}, u32[]{:S(2)}) %copy-start.1) | copy-done | bytes 3670040
  7.9 0.4 multiply_convert_fusion.nin_ref
  8.3 1.0 copy-done.5
  9.4 1.4 fusion.5
  10.8 2.0 %select_reduce_fusion = (f32[128]{0:T(128)S(1)}, f32[128,8]{1,0:T(8,128)S(1)}) fusion(f32[128,256]{1,0:T(8,128)S(1)} %fusion.5, s32[128,8]{1,0:T(8,128)S(1)} %copy.30), kind=kLoop, calls=%fused_computation.11 | loop fusion | flops 1047424 | bytes 139776 | tf_op jit(solution)/shard_map/reduce_sum | solution.py:504
  13.0 0.1 fusion.7
  13.2 0.7 fusion.13
  14.0 7.3 %copy.36 = bf16[896,8,2,256]{3,1,2,0:T(8,128)(2,1)} copy(bf16[896,8,2,256]{3,2,1,0:T(2,128)(2,1)} %bitcast.46) | data formatting | bytes 14680064
  21.3 105.9 %shard_map.139 = bf16[128,3712]{1,0:T(8,128)(2,1)} custom-call(bf16[128,128]{1,0:T(8,128)(2,1)} %get-tuple-element.10.p_in_ref, bf16[128,128]{1,0:T(8,128)(2,1)} %get-tuple-element.9.p_gr_ref, bf16[96,128]{1,0:T(8,128)(2,1)} %constant.37.clone.q_ref, bf16[2,128,48]{2,1,0:T(8,128)(2,1)} %constant.38.clone.qt_ref, bf16[128,7168]{1,0:T(8,128)(2,1)} %copy-done.4, ...), custom_call_target="tpu_custom_call" | custom-call | tf_op jit(solution)/shard_map/pallas_call | solution.py:302
  127.3 0.9 convert_reduce_fusion
  128.6 0.4 select_reduce_fusion.2
  129.1 1.9 %fusion.8 = f32[128,3584]{1,0:T(8,128)S(1)} fusion(bf16[128,128]{1,0:T(8,128)(2,1)S(1)} %get-tuple-element.8, bf16[128,3712]{1,0:T(8,128)(2,1)} %shard_map.139), kind=kOutput, calls=%fused_computation.25 | convolution fusion | flops 117440512 | bytes 2785280 | tf_op jit(solution)/shard_map/dot_general | solution.py:31
  131.0 0.4 fusion.10
  131.5 3.6 %multiply_reduce_fusion = (f32[128]{0:T(128)S(1)}, f32[128,7168]{1,0:T(8,128)S(1)}) fusion(f32[128,7168]{1,0:T(8,128)S(1)} %copy-done.2, f32[128]{0:T(128)S(1)} %add_rsqrt_fusion, f32[7168]{0:T(1024)S(1)} %copy-done.10, bf16[128,256]{1,0:T(8,128)(2,1)S(1)} %select_reduce_fusion.2, bf16[256,7168]{1,0:T(8,128)(2,1)} %param.18, f32[128,3584]{1,0:T(8,128)S(1)} %fusion.8, ...), kind=kOutput, calls=%fused_computation.8 | convolution fusion | flops 475266944 | bytes 14775296 | tf_op jit(solution)/shard_map/dot_general | solution.py:562
  135.1 1.0 add_convert_fusion
  136.2 0.4 fusion.2
  136.5 4.6 %convolution_convert_fusion = bf16[16,16384]{1,0:T(8,128)(2,1)S(1)} fusion(bf16[128,16384]{1,0:T(8,128)(2,1)} %param.13, bf16[128,7168]{1,0:T(8,128)(2,1)S(1)} %add_convert_fusion, bf16[16,7168]{1,0:T(8,128)(2,1)S(1)} %copy-done.9), kind=kOutput, calls=%fused_computation | convolution fusion | flops 96735232 | bytes 6782976 | tf_op jit(solution)/shard_map/tr,th->rh/dot_general | solution.py:580
  141.2 1.0 maximum_maximum_fusion.x_ref
  142.2 28.0 %shard_map.140 = bf16[16,24576]{1,0:T(8,128)(2,1)} custom-call(bf16[16,24576]{1,0:T(8,128)(2,1)} %maximum_maximum_fusion.x_ref), custom_call_target="tpu_custom_call" | custom-call | tf_op jit(solution)/shard_map/pallas_call | solution.py:410
  170.2 2.1 %convert_multiply_fusion = f32[16,16384]{1,0:T(8,128)} fusion(bf16[16,24576]{1,0:T(8,128)(2,1)} %shard_map.140), kind=kLoop, calls=%fused_computation.22 | loop fusion | flops 524288 | bytes 1572864 | tf_op jit(solution)/shard_map/div | solution.py:422
  172.3 1.7 convert_multiply_fusion.1
  (42 shorter events, 0.9 us)
Async XLA Ops:
  0.6 1.0 copy-start
  0.6 4.4 %copy-start.9 = (bf16[16,7168]{1,0:T(8,128)(2,1)S(1)}, bf16[16,7168]{1,0:T(8,128)(2,1)}, u32[]{:S(2)}) copy-start(bf16[16,7168]{1,0:T(8,128)(2,1)} %param.16) | copy-start | bytes 688132
  0.7 4.4 %copy-start.8 = (bf16[128,7168]{1,0:T(8,128)(2,1)S(1)}, bf16[128,7168]{1,0:T(8,128)(2,1)}, u32[]{:S(2)}) copy-start(bf16[128,7168]{1,0:T(8,128)(2,1)} %param.12) | copy-start | bytes 5505028
  5.1 2.8 %copy-start.10 = (f32[7168]{0:T(1024)S(1)}, f32[7168]{0:T(1024)}, u32[]{:S(2)}) copy-start(f32[7168]{0:T(1024)} %param.17) | copy-start | bytes 86020
  6.0 1.9 %copy-start.1 = (f32[128,7168]{1,0:T(8,128)}, f32[128,7168]{1,0:T(8,128)S(1)}, u32[]{:S(2)}) copy-start(f32[128,7168]{1,0:T(8,128)S(1)} %get-tuple-element.12) | copy-start | bytes 11010052
  6.0 3.4 %copy-start.5 = (bf16[256,7168]{1,0:T(8,128)(2,1)S(1)}, bf16[256,7168]{1,0:T(8,128)(2,1)}, u32[]{:S(2)}) copy-start(bf16[256,7168]{1,0:T(8,128)(2,1)} %param.18) | copy-start | bytes 11010052
  9.3 12.0 %copy-start.4 = (bf16[128,7168]{1,0:T(8,128)(2,1)}, bf16[128,7168]{1,0:T(8,128)(2,1)S(1)}, u32[]{:S(2)}) copy-start(bf16[128,7168]{1,0:T(8,128)(2,1)S(1)} %multiply_convert_fusion.nin_ref) | copy-start | bytes 5505028
  9.3 1.4 copy-start.11
  127.3 3.7 %copy-start.6 = (bf16[128,3712]{1,0:T(8,128)(2,1)S(1)}, bf16[128,3712]{1,0:T(8,128)(2,1)}, u32[]{:S(2)}) copy-start(bf16[128,3712]{1,0:T(8,128)(2,1)} %shard_map.139) | copy-start | bytes 2850820
  128.6 2.8 %copy-start.2 = (f32[128,7168]{1,0:T(8,128)S(1)}, f32[128,7168]{1,0:T(8,128)}, u32[]{:S(2)}) copy-start(f32[128,7168]{1,0:T(8,128)} %copy-done.1) | copy-start | bytes 11010052
  131.4 3.7 %copy-start.7 = (bf16[128,7168]{1,0:T(8,128)(2,1)S(1)}, bf16[128,7168]{1,0:T(8,128)(2,1)}, u32[]{:S(2)}) copy-start(bf16[128,7168]{1,0:T(8,128)(2,1)} %cot_ref.1) | copy-start | bytes 5505028
  136.2 5.0 %copy-start.3 = (bf16[128,7168]{1,0:T(8,128)(2,1)}, bf16[128,7168]{1,0:T(8,128)(2,1)S(1)}, u32[]{:S(2)}) copy-start(bf16[128,7168]{1,0:T(8,128)(2,1)S(1)} %add_convert_fusion) | copy-start | bytes 5505028

commit v3 on v2

--- a/solution.py
+++ b/solution.py
@@ -73,7 +73,6 @@
     parts,
     arrived,
     back,
-    back_got,
     wj,
     wd,
     w_sem,
@@ -121,7 +120,9 @@
         first.append(copies)
 
     second, relayed = [], []
-    for c in range(CHUNKS + 1):
+    projected = jnp.zeros((n_dp * slots, 2 * quarter), F32)
+    hidden_grad = jnp.zeros((n_dp * slots, quarter), F32)
+    for c in range(CHUNKS + 2):
         if c < CHUNKS:
             cols = pl.ds(c * step, step)
             for copy in first[c]:
@@ -141,7 +142,7 @@
                     for j in (1, 2)
                 ]
             )
-        if c > 0:
+        if 0 < c <= CHUNKS:
             cols = pl.ds((c - 1) * step, step)
             copies = []
             for j in (1, 2):
@@ -157,18 +158,17 @@
                     )
                 )
             relayed.append(copies)
-    load_j.wait()
-    load_d.wait()
-    projected = jnp.zeros((n_dp * slots, 2 * quarter), F32)
-    hidden_grad = jnp.zeros((n_dp * slots, quarter), F32)
-    for c in range(CHUNKS):
-        cols = pl.ds(c * step, step)
-        for copy in relayed[c]:
-            copy.wait_recv()
-        rows_in = rows[:, :slots, cols].reshape(n_dp * slots, step)
-        rows_grad = rows[:, slots:, cols].reshape(n_dp * slots, step)
-        projected += jnp.dot(rows_in, wj[cols, :], preferred_element_type=F32)
-        hidden_grad += dot_nt(rows_grad, wd[:, cols])
+        if c == 2:
+            load_j.wait()
+            load_d.wait()
+        if c >= 2:
+            cols = pl.ds((c - 2) * step, step)
+            for copy in relayed[c - 2]:
+                copy.wait_recv()
+            rows_in = rows[:, :slots, cols].reshape(n_dp * slots, step)
+            rows_grad = rows[:, slots:, cols].reshape(n_dp * slots, step)
+            projected += jnp.dot(rows_in, wj[cols, :], preferred_element_type=F32)
+            hidden_grad += dot_nt(rows_grad, wd[:, cols])
     gate_pre = projected[:, :quarter]
     up_pre = projected[:, quarter:]
     sigma_gate = jax.nn.sigmoid(gate_pre)
@@ -253,19 +253,17 @@
                 copies.append(
                     remote(
                         back.at[theirs, cols],
-                        back_got.at[mine, cols],
+                        out_ref.at[mine, cols],
                         b_send.at[c, j - 1],
                         b_recv.at[c, j - 1],
                         (d, e ^ j),
                     )
                 )
-            back_got[mine, cols] = back[mine, cols]
+            out_ref[mine, cols] = back[mine, cols]
             fourth.append(copies)
-    for c, (_, size, low, real) in enumerate(spans):
-        for copy in fourth[c]:
+    for copies in fourth:
+        for copy in copies:
             copy.wait_recv()
-        cols = pl.ds(low, size)
-        out_ref[:, cols] = back_got[:, cols]
     third = [sum(copies, []) for copies in third]
     for stage in (first, second, relayed, third, passed, fourth):
         for copies in stage:
@@ -281,7 +279,6 @@
         ((n_dp, 2 * slots, width), BF16),
         ((n_dp, slots, width + LANES), BF16),
         ((n_dp - 1, slots, width + LANES), BF16),
-        ((padded, width // 2 + LANES), BF16),
         ((padded, width // 2 + LANES), BF16),
         ((width, 2 * quarter), BF16),
         ((quarter, width), BF16),

time: 174 us -> 174 us (level)
  no operation moved by 1% of the time
where the time goes in v3:
time: 174 us
  Pallas kernels  134 us (77%)
  matrix products  16.7 us (10%)
  local copies, waits for them, and re-layouts  11.8 us (7%)
  other arithmetic  10.7 us (6%)
    pallas_call x1, Pallas kernels, expert_exchange(): pl.pallas_call(functools.partial(expert_kernel, n_dp, n_exp), out_shape=j...  106 us
    pallas_call x1, Pallas kernels, mean_over_devices(): pl.pallas_call(functools.partial(reduce_kernel, n_dp, n_exp), out_shape=j...  28 us
    unnamed x26, local copies, waits for them, and re-layouts  11.4 us
    dot_general x1, matrix products, local(): jnp.einsum('tr,th->rh', hidden_code_gradient, heads_out, preferred_elemen...  4.63 us
    div x2, other arithmetic, mean_over_devices(): outs.append(out[:, at:at + t.shape[1]].astype(F32) / devices)  3.82 us
    dot_general x1, matrix products, local(): jnp.dot(logit_grad, router, preferred_element_type=jnp.float32)  3.64 us

profile of v3, /device:TPU:0, one launch (start us, length us, event | category | flops | bytes accessed | tf_op | source)
XLA Modules:
  0.0 174.0 jit_solution(5349725501711713040)
XLA Ops:
  0.7 1.0 copy-done
  1.7 3.4 %convolution_convert_fusion.1 = bf16[128,16]{0,1:T(8,128)(2,1)S(1)} fusion(bf16[128,16384]{1,0:T(8,128)(2,1)} %param.13, bf16[16,16384]{1,0:T(8,128)(2,1)S(1)} %copy-done), kind=kOutput, calls=%fused_computation.19 | convolution fusion | flops 67110912 | bytes 4722688 | tf_op jit(solution)/shard_map/th,rh->tr/dot_general | solution.py:486
  5.1 0.9 multiply_reduce_fusion.1
  6.0 1.9 %copy-done.1 = f32[128,7168]{1,0:T(8,128)} copy-done((f32[128,7168]{1,0:T(8,128)}, f32[128,7168]{1,0:T(8,128)S(1)}, u32[]{:S(2)}) %copy-start.1) | copy-done | bytes 3670040
  7.9 0.4 multiply_convert_fusion.nin_ref
  8.3 1.0 copy-done.5
  9.4 1.4 fusion.5
  10.8 2.0 %select_reduce_fusion = (f32[128]{0:T(128)S(1)}, f32[128,8]{1,0:T(8,128)S(1)}) fusion(f32[128,256]{1,0:T(8,128)S(1)} %fusion.5, s32[128,8]{1,0:T(8,128)S(1)} %copy.30), kind=kLoop, calls=%fused_computation.11 | loop fusion | flops 1047424 | bytes 139776 | tf_op jit(solution)/shard_map/reduce_sum | solution.py:501
  13.0 0.1 fusion.7
  13.2 0.7 fusion.13
  14.0 7.3 %copy.36 = bf16[896,8,2,256]{3,1,2,0:T(8,128)(2,1)} copy(bf16[896,8,2,256]{3,2,1,0:T(2,128)(2,1)} %bitcast.46) | data formatting | bytes 14680064
  21.3 105.9 %shard_map.139 = bf16[128,3712]{1,0:T(8,128)(2,1)} custom-call(bf16[128,128]{1,0:T(8,128)(2,1)} %get-tuple-element.10.p_in_ref, bf16[128,128]{1,0:T(8,128)(2,1)} %get-tuple-element.9.p_gr_ref, bf16[96,128]{1,0:T(8,128)(2,1)} %constant.37.clone.q_ref, bf16[2,128,48]{2,1,0:T(8,128)(2,1)} %constant.38.clone.qt_ref, bf16[128,7168]{1,0:T(8,128)(2,1)} %copy-done.4, ...), custom_call_target="tpu_custom_call" | custom-call | tf_op jit(solution)/shard_map/pallas_call | solution.py:299
  127.2 0.9 convert_reduce_fusion
  128.6 0.4 select_reduce_fusion.2
  129.1 1.9 %fusion.8 = f32[128,3584]{1,0:T(8,128)S(1)} fusion(bf16[128,128]{1,0:T(8,128)(2,1)S(1)} %get-tuple-element.8, bf16[128,3712]{1,0:T(8,128)(2,1)} %shard_map.139), kind=kOutput, calls=%fused_computation.25 | convolution fusion | flops 117440512 | bytes 2785280 | tf_op jit(solution)/shard_map/dot_general | solution.py:31
  131.0 0.4 fusion.10
  131.4 3.6 %multiply_reduce_fusion = (f32[128]{0:T(128)S(1)}, f32[128,7168]{1,0:T(8,128)S(1)}) fusion(f32[128,7168]{1,0:T(8,128)S(1)} %copy-done.2, f32[128]{0:T(128)S(1)} %add_rsqrt_fusion, f32[7168]{0:T(1024)S(1)} %copy-done.10, bf16[128,256]{1,0:T(8,128)(2,1)S(1)} %select_reduce_fusion.2, bf16[256,7168]{1,0:T(8,128)(2,1)} %param.18, f32[128,3584]{1,0:T(8,128)S(1)} %fusion.8, ...), kind=kOutput, calls=%fused_computation.8 | convolution fusion | flops 475266944 | bytes 14775296 | tf_op jit(solution)/shard_map/dot_general | solution.py:559
  135.1 1.0 add_convert_fusion
  136.1 0.4 fusion.2
  136.5 4.6 %convolution_convert_fusion = bf16[16,16384]{1,0:T(8,128)(2,1)S(1)} fusion(bf16[128,16384]{1,0:T(8,128)(2,1)} %param.13, bf16[128,7168]{1,0:T(8,128)(2,1)S(1)} %add_convert_fusion, bf16[16,7168]{1,0:T(8,128)(2,1)S(1)} %copy-done.9), kind=kOutput, calls=%fused_computation | convolution fusion | flops 96735232 | bytes 6782976 | tf_op jit(solution)/shard_map/tr,th->rh/dot_general | solution.py:577
  141.1 1.0 maximum_maximum_fusion.x_ref
  142.2 28.0 %shard_map.140 = bf16[16,24576]{1,0:T(8,128)(2,1)} custom-call(bf16[16,24576]{1,0:T(8,128)(2,1)} %maximum_maximum_fusion.x_ref), custom_call_target="tpu_custom_call" | custom-call | tf_op jit(solution)/shard_map/pallas_call | solution.py:407
  170.2 2.1 %convert_multiply_fusion = f32[16,16384]{1,0:T(8,128)} fusion(bf16[16,24576]{1,0:T(8,128)(2,1)} %shard_map.140), kind=kLoop, calls=%fused_computation.22 | loop fusion | flops 524288 | bytes 1572864 | tf_op jit(solution)/shard_map/div | solution.py:419
  172.2 1.7 convert_multiply_fusion.1
  (42 shorter events, 0.9 us)
Async XLA Ops:
  0.6 1.0 copy-start
  0.6 4.4 %copy-start.9 = (bf16[16,7168]{1,0:T(8,128)(2,1)S(1)}, bf16[16,7168]{1,0:T(8,128)(2,1)}, u32[]{:S(2)}) copy-start(bf16[16,7168]{1,0:T(8,128)(2,1)} %param.16) | copy-start | bytes 688132
  0.7 4.4 %copy-start.8 = (bf16[128,7168]{1,0:T(8,128)(2,1)S(1)}, bf16[128,7168]{1,0:T(8,128)(2,1)}, u32[]{:S(2)}) copy-start(bf16[128,7168]{1,0:T(8,128)(2,1)} %param.12) | copy-start | bytes 5505028
  5.1 2.8 %copy-start.10 = (f32[7168]{0:T(1024)S(1)}, f32[7168]{0:T(1024)}, u32[]{:S(2)}) copy-start(f32[7168]{0:T(1024)} %param.17) | copy-start | bytes 86020
  6.0 1.9 %copy-start.1 = (f32[128,7168]{1,0:T(8,128)}, f32[128,7168]{1,0:T(8,128)S(1)}, u32[]{:S(2)}) copy-start(f32[128,7168]{1,0:T(8,128)S(1)} %get-tuple-element.12) | copy-start | bytes 11010052
  6.0 3.4 %copy-start.5 = (bf16[256,7168]{1,0:T(8,128)(2,1)S(1)}, bf16[256,7168]{1,0:T(8,128)(2,1)}, u32[]{:S(2)}) copy-start(bf16[256,7168]{1,0:T(8,128)(2,1)} %param.18) | copy-start | bytes 11010052
  9.3 12.0 %copy-start.4 = (bf16[128,7168]{1,0:T(8,128)(2,1)}, bf16[128,7168]{1,0:T(8,128)(2,1)S(1)}, u32[]{:S(2)}) copy-start(bf16[128,7168]{1,0:T(8,128)(2,1)S(1)} %multiply_convert_fusion.nin_ref) | copy-start | bytes 5505028
  9.3 1.4 copy-start.11
  127.2 3.7 %copy-start.6 = (bf16[128,3712]{1,0:T(8,128)(2,1)S(1)}, bf16[128,3712]{1,0:T(8,128)(2,1)}, u32[]{:S(2)}) copy-start(bf16[128,3712]{1,0:T(8,128)(2,1)} %shard_map.139) | copy-start | bytes 2850820
  128.6 2.8 %copy-start.2 = (f32[128,7168]{1,0:T(8,128)S(1)}, f32[128,7168]{1,0:T(8,128)}, u32[]{:S(2)}) copy-start(f32[128,7168]{1,0:T(8,128)} %copy-done.1) | copy-start | bytes 11010052
  131.4 3.7 %copy-start.7 = (bf16[128,7168]{1,0:T(8,128)(2,1)S(1)}, bf16[128,7168]{1,0:T(8,128)(2,1)}, u32[]{:S(2)}) copy-start(bf16[128,7168]{1,0:T(8,128)(2,1)} %cot_ref.1) | copy-start | bytes 5505028
  136.1 5.0 %copy-start.3 = (bf16[128,7168]{1,0:T(8,128)(2,1)}, bf16[128,7168]{1,0:T(8,128)(2,1)S(1)}, u32[]{:S(2)}) copy-start(bf16[128,7168]{1,0:T(8,128)(2,1)S(1)} %add_convert_fusion) | copy-start | bytes 5505028
